TPU v7x, 256 devices: a whole 4x4x8 slice. The times are simulated.
256 devices in a mesh: dp: 16 (over x, y), fsdp: 16 (over z, core).
Axes of the slice: x: 4, y: 4, z: 8, core: 2. Of those that a mesh axis runs over, the one named last changes fastest.
Arguments:
- stream: bfloat16 [131072, 4096], P(('dp', 'fsdp')), may hold values from -6 to 6
- lengths: int32 [256, 2], P(('dp', 'fsdp')), may hold values from 192 to 320, as said below
- partner: int32 [512], P(('dp', 'fsdp')), may hold values from 0 to 511, each once
- norm_gain: bfloat16 [4096], replicated, may hold values from 0.25 to 1.75
- w_query: bfloat16 [4096, 2048], P('fsdp'), may hold values from -0.09375 to 0.09375
- key_weight: bfloat16 [4096, 512], P('fsdp'), may hold values from -0.09375 to 0.09375
- value_weight: bfloat16 [4096, 512], P('fsdp'), may hold values from -0.09375 to 0.09375
- w_out: bfloat16 [2048, 4096], P('fsdp'), may hold values from -0.125 to 0.125
- q_gain: bfloat16 [128], replicated, may hold values from 0.099609375 to 1.8984375
- key_norm_gain: bfloat16 [128], replicated, may hold values from 0.099609375 to 1.8984375
- final_gain: bfloat16 [4096], replicated, may hold values from 0.099609375 to 1.8984375
Outputs:
- embed_grad: float32 [512, 4096], P(('dp', 'fsdp'))
- loss: float32 [], replicated
Inputs may be any that keep to these rules, and one draw needn't show every extreme that they name: `lengths`: each device's row sums to 512; some device holds a text of exactly 320 tokens. `partner`: each index appears once.
All inputs are finite; a program needn't handle non-finite values.
Results may differ from a plain program's by a relative error of at most 0.004.
Values may be sent and summed in bfloat16 or wider, within the bound.
A program may use at most 128 MiB of HBM per device.

v0:
```python
import math

import jax
import jax.numpy as jnp
from jax import lax
from jax.sharding import PartitionSpec as P

QUERY_HEADS = 16
KEY_VALUE_HEADS = 4
HEAD_SIZE = 128


EPS = 1e-06
THETA = 1000000.0
TEMPER = 0.05


def per_head_norm(value_rows, gain):
    square = jnp.mean(value_rows * value_rows, axis=-1, keepdims=True)
    return value_rows * lax.rsqrt(square + EPS) * gain.astype(jnp.float32)


def apply_rotary(value_rows, token_position):
    half = value_rows.shape[-1] // 2
    freq = THETA ** (-jnp.arange(half, dtype=jnp.float32) * 2.0 / value_rows.shape[-1])
    angle = token_position.astype(jnp.float32)[:, None, None] * freq[None, None, :]
    cosine = jnp.cos(angle)
    sine = jnp.sin(angle)
    first = value_rows[..., :half]
    second = value_rows[..., half:]
    return jnp.concatenate(
        [first * cosine - second * sine, second * cosine + first * sine], axis=-1
    )


def layout(lengths, token_count):
    ends = jnp.cumsum(lengths)
    starts = ends - lengths
    place = jnp.arange(token_count, dtype=jnp.int32)
    member = (place[:, None] >= starts[None, :]) & (place[:, None] < ends[None, :])
    first = jnp.sum(jnp.where(member, starts[None, :], 0), axis=1)
    return (member, place - first, ends - 1)


def local(
    stream,
    lengths,
    partner,
    norm_gain,
    w_query,
    key_weight,
    value_weight,
    w_out,
    q_gain,
    key_norm_gain,
    final_gain,
):
    token_count = stream.shape[0]
    seq_len = lengths[0]
    sequence_batch = seq_len.shape[0]
    member, token_position, last = layout(seq_len, token_count)
    flat = stream.astype(jnp.float32)
    normalized = (
        flat
        * lax.rsqrt(jnp.mean(flat * flat, axis=-1, keepdims=True) + EPS)
        * norm_gain.astype(jnp.float32)
    ).astype(jnp.bfloat16)
    columns = normalized
    key_rows = jnp.dot(
        columns,
        lax.all_gather(key_weight, "fsdp", axis=0, tiled=True),
        preferred_element_type=jnp.float32,
    )
    value_rows = jnp.dot(
        columns,
        lax.all_gather(value_weight, "fsdp", axis=0, tiled=True),
        preferred_element_type=jnp.float32,
    )
    key_rows = apply_rotary(
        per_head_norm(key_rows.reshape(token_count, KEY_VALUE_HEADS, HEAD_SIZE), key_norm_gain),
        token_position,
    ).astype(jnp.bfloat16)
    value_rows = value_rows.astype(jnp.bfloat16).reshape(token_count, KEY_VALUE_HEADS, HEAD_SIZE)
    lane = lax.axis_index("fsdp")
    pooled = jnp.take(normalized, last, axis=0)
    width_shard = w_query.shape[0]
    all_pooled = lax.all_gather(pooled, "fsdp", axis=0, tiled=True)
    own_width = lax.dynamic_slice_in_dim(all_pooled, lane * width_shard, width_shard, 1)
    query_rows = lax.psum_scatter(
        jnp.dot(own_width, w_query, preferred_element_type=jnp.float32),
        "fsdp",
        scatter_dimension=0,
        tiled=True,
    ).reshape(sequence_batch, QUERY_HEADS, HEAD_SIZE)
    query_rows = apply_rotary(per_head_norm(query_rows, q_gain), seq_len - 1).astype(jnp.bfloat16)
    query_rows = query_rows.reshape(
        sequence_batch, KEY_VALUE_HEADS, QUERY_HEADS // KEY_VALUE_HEADS, HEAD_SIZE
    )
    scores = jnp.einsum(
        "skgd,tkd->skgt", query_rows, key_rows, preferred_element_type=jnp.float32
    ) / math.sqrt(HEAD_SIZE)
    inside = member.T.astype(jnp.float32)[:, None, None, :]
    weights = jnp.exp(scores) * inside
    probs = (weights / jnp.sum(weights, axis=-1, keepdims=True)).astype(jnp.bfloat16)
    mixed = jnp.einsum("skgt,tkd->skgd", probs, value_rows, preferred_element_type=jnp.float32)
    mixed = mixed.reshape(sequence_batch, QUERY_HEADS * HEAD_SIZE).astype(jnp.bfloat16)
    head_shard = w_out.shape[0]
    all_mixed = lax.all_gather(mixed, "fsdp", axis=0, tiled=True)
    own_heads = lax.dynamic_slice_in_dim(all_mixed, lane * head_shard, head_shard, 1)
    state = jnp.take(stream, last, axis=0).astype(jnp.float32) + lax.psum_scatter(
        jnp.dot(own_heads, w_out, preferred_element_type=jnp.float32),
        "fsdp",
        scatter_dimension=0,
        tiled=True,
    )
    scaled = (
        state
        * lax.rsqrt(jnp.mean(state * state, axis=-1, keepdims=True) + EPS)
        * final_gain.astype(jnp.float32)
    )
    embedding = (scaled / jnp.sqrt(jnp.sum(scaled * scaled, axis=-1, keepdims=True) + EPS)).astype(
        jnp.bfloat16
    )
    everyone = lax.all_gather(embedding, ("dp", "fsdp"), axis=0, tiled=True)
    texts = everyone.shape[0]
    offset = lax.axis_index(("dp", "fsdp")) * sequence_batch
    sim = jnp.dot(embedding, everyone.T, preferred_element_type=jnp.float32) / TEMPER
    columns = jnp.arange(texts, dtype=jnp.int32)
    own_rows = offset + jnp.arange(sequence_batch, dtype=jnp.int32)
    hit = columns[None, :] == partner[:, None]
    keep = (columns[None, :] != own_rows[:, None]) | hit
    weights_row = jnp.where(keep, jnp.exp(sim), 0.0)
    total = jnp.sum(weights_row, axis=1)
    target = jnp.sum(jnp.where(hit, sim, 0.0), axis=1)
    loss = lax.psum(jnp.sum(jnp.log(total) - target), ("dp", "fsdp")) / texts
    pull = (weights_row / total[:, None] - hit.astype(jnp.float32)).astype(jnp.bfloat16)
    row_part = jnp.dot(pull, everyone, preferred_element_type=jnp.float32)
    column_part = lax.psum_scatter(
        jnp.einsum("sn,sd->nd", pull, embedding, preferred_element_type=jnp.float32),
        ("dp", "fsdp"),
        scatter_dimension=0,
        tiled=True,
    )
    embed_grad = (column_part + row_part) / TEMPER
    return (embed_grad, loss)


def solution(mesh):
    return jax.shard_map(
        local,
        mesh=mesh,
        in_specs=(
            P(("dp", "fsdp"), None),
            P(("dp", "fsdp"), None),
            P(("dp", "fsdp")),
            P(),
            P("fsdp", None),
            P("fsdp", None),
            P("fsdp", None),
            P("fsdp", None),
            P(),
            P(),
            P(),
        ),
        out_specs=(P(("dp", "fsdp"), None), P()),
        check_vma=False,
    )
```

profile of v0, /device:TPU:1, one launch (start us, length us, event | category | flops | bytes accessed | tf_op | source)
XLA Modules:
  0.0 789.7 jit_solution(6586374141562280058)
XLA Ops:
  7.2 0.9 reduce-window.4
  8.2 3.2 fusion
  11.4 0.2 copy-done.1
  11.6 3.6 fusion.2
  15.2 3.3 gather_fusion.1
  18.5 0.1 fusion.16
  18.6 22.0 %all-gather = bf16[16,2,4096]{2,1,0:T(2,128)(2,1)S(1)} all-gather(bf16[1,2,4096]{2,1,0:T(2,128)(2,1)S(1)} %fusion.16), channel_id=1, replica_groups=mesh['dp'=16,'fsdp'=16] {'fsdp'}, dimensions={0}, use_global_device_ids=true | all-gather | bytes 278528 | tf_op jit(solution)/shard_map/all_gather | solution.py:87
  40.6 0.1 reshape.288
  40.7 1.0 fusion.14
  41.8 0.7 all-gather.9.cloned.1.call-update
  42.5 0.7 all-gather.7.cloned.1.call-update
  43.3 0.6 dynamic-slice
  44.6 0.1 fusion.23
  44.7 0.1 multiply_cosine_fusion.1
  44.8 0.1 and_convert_fusion
  44.9 1.0 multiply_cosine_fusion
  45.9 102.2 %all-reduce.7.cloned.1.call-done = f32[32,2048]{1,0:T(8,128)} async-done(((f32[32,2048]{1,0:T(8,128)}), f32[32,2048]{1,0:T(8,128)}) %all-reduce.7.cloned.1.call-update) | async-done | bytes 262160
  148.1 0.8 dynamic-slice_bitcast_fusion
  148.9 0.1 fusion.12
  149.0 0.1 fusion.13
  149.1 0.1 subtract_convert_fusion.1
  149.2 43.8 %all-gather.9.cloned.1.call-done = bf16[4096,512]{1,0:T(8,128)(2,1)} async-done(((bf16[256,512]{1,0:T(8,128)(2,1)}), bf16[4096,512]{1,0:T(8,128)(2,1)}) %all-gather.9.cloned.1.call-update) | async-done | bytes 4194320 | tf_op jit(solution)/shard_map/all_gather | solution.py:71
  193.0 6.9 multiply_reduce_fusion
  199.9 1.5 copy.25
  201.4 0.3 multiply_multiply_fusion
  201.8 0.4 subtract_convert_fusion
  202.2 0.4 fusion.6
  202.6 33.0 %all-gather.7.cloned.1.call-done = bf16[4096,512]{1,0:T(8,128)(2,1)} async-done(((bf16[256,512]{1,0:T(8,128)(2,1)}), bf16[4096,512]{1,0:T(8,128)(2,1)}) %all-gather.7.cloned.1.call-update) | async-done | bytes 4194320 | tf_op jit(solution)/shard_map/all_gather | solution.py:76
  235.7 5.8 convolution_convert_fusion
  241.5 0.3 fusion.7
  241.8 16.7 %all-gather.1 = bf16[16,2,2048]{2,1,0:T(2,128)(2,1)S(1)} all-gather(bf16[1,2,2048]{2,1,0:T(2,128)(2,1)S(1)} %reshape.289), channel_id=1, replica_groups=mesh['dp'=16,'fsdp'=16] {'fsdp'}, dimensions={0}, use_global_device_ids=true | all-gather | bytes 139264 | tf_op jit(solution)/shard_map/all_gather | solution.py:108
  258.6 0.1 reshape.290
  258.6 1.1 fusion.18
  259.7 0.0 all-gather.11.cloned.1.call-start
  259.8 3.3 gather_fusion
  263.1 104.8 %all-reduce.9.cloned.1.call-done = f32[32,4096]{1,0:T(8,128)} async-done(((f32[32,4096]{1,0:T(8,128)}), f32[32,4096]{1,0:T(8,128)}) %all-reduce.9.cloned.1.call-update) | async-done | bytes 524304
  368.0 1.1 multiply_reduce_fusion.2
  369.1 0.2 multiply_reduce_fusion.1
  369.3 0.7 fusion.49
  370.1 0.0 all-reduce.11.cloned.1.call-start
  370.1 118.0 %all-gather.11.cloned.1.call-done = bf16[256,2,4096]{2,1,0:T(2,128)(2,1)} async-done(((bf16[1,2,4096]{2,1,0:T(2,128)(2,1)}), bf16[256,2,4096]{2,1,0:T(2,128)(2,1)}) %all-gather.11.cloned.1.call-update) | async-done | bytes 4194320 | tf_op jit(solution)/shard_map/all_gather | solution.py:124
  488.1 7.2 reshape.292
  495.3 3.5 select_reduce_fusion
  498.9 4.6 fusion.34
  503.5 0.6 subtract_reduce_fusion
  504.1 75.3 %psum.7 = f32[]{:T(128)} all-reduce(f32[]{:T(128)} %subtract_reduce_fusion), channel_id=1, replica_groups=mesh['dp'=16,'fsdp'=16] {'dp','fsdp'}, use_global_device_ids=true, to_apply=%region_14.16 | all-reduce | flops 1 | bytes 8 | tf_op jit(solution)/shard_map/psum | solution.py:135
  580.0 198.2 %all-reduce.11.cloned.1.call-done = f32[512,4096]{1,0:T(8,128)} async-done(((f32[512,4096]{1,0:T(8,128)}), f32[512,4096]{1,0:T(8,128)}) %all-reduce.11.cloned.1.call-update) | async-done | bytes 8388624
  778.2 3.5 fusion.3
  (44 shorter events, 0.4 us)
Async XLA Ops:
  7.2 251.4 %copy-start = (bf16[128,4096]{1,0:T(8,128)(2,1)S(1)}, bf16[128,4096]{1,0:T(8,128)(2,1)}, u32[]{:S(2)}) copy-start(bf16[128,4096]{1,0:T(8,128)(2,1)} %param.20) | copy-start | bytes 3145732
  7.2 4.2 copy-start.4
  7.2 140.9 %all-reduce.7.cloned.1.call-start = ((), (), s32[]{:S(2)}) async-start(), calls=%async_computation.3 | async-start | bytes 524288
  8.1 3.4 copy-start.1
  11.6 29.1 %copy-start.2 = (bf16[256,2048]{1,0:T(8,128)(2,1)S(1)}, bf16[256,2048]{1,0:T(8,128)(2,1)}, u32[]{:S(2)}) copy-start(bf16[256,2048]{1,0:T(8,128)(2,1)} %param.17) | copy-start | bytes 3145732
  11.6 31.7 %copy-start.7 = (bf16[128]{0:T(256)(128)(2,1)S(1)}, bf16[128]{0:T(256)(128)(2,1)}, u32[]{:S(2)}) copy-start(bf16[128]{0:T(256)(128)(2,1)} %param.21) | copy-start | bytes 772
  11.6 31.7 %copy-start.8 = (bf16[128]{0:T(256)(128)(2,1)S(1)}, bf16[128]{0:T(256)(128)(2,1)}, u32[]{:S(2)}) copy-start(bf16[128]{0:T(256)(128)(2,1)} %param.22) | copy-start | bytes 772
  11.6 31.7 %copy-start.9 = (u32[256]{0:T(256)S(1)}, u32[256]{0:T(256)}, u32[]{:S(2)}) copy-start(u32[256]{0:T(256)} %constant.77) | copy-start | bytes 3076
  11.6 33.0 %copy-start.6 = (s32[1,2]{1,0:T(1,128)S(1)}, s32[1,2]{1,0:T(1,128)}, u32[]{:S(2)}) copy-start(s32[1,2]{1,0:T(1,128)} %param.14) | copy-start | bytes 28
  41.7 151.2 %all-gather.9.cloned.1.call-start = ((), (), s32[]{:S(2)}) async-start(), calls=%async_computation.1 | async-start | bytes 4456448 | tf_op jit(solution)/shard_map/all_gather | solution.py:71
  42.5 193.2 %all-gather.7.cloned.1.call-start = ((), (), s32[]{:S(2)}) async-start(), calls=%async_computation | async-start | bytes 4456448 | tf_op jit(solution)/shard_map/all_gather | solution.py:76
  43.2 324.7 %all-reduce.9.cloned.1.call-start = ((), (), s32[]{:S(2)}) async-start(), calls=%async_computation.4 | async-start | bytes 1048576
  202.6 60.5 %copy-start.5 = (bf16[4096]{0:T(1024)(128)(2,1)S(1)}, bf16[4096]{0:T(1024)(128)(2,1)}, u32[]{:S(2)}) copy-start(bf16[4096]{0:T(1024)(128)(2,1)} %param.23) | copy-start | bytes 24580
  259.7 228.4 %all-gather.11.cloned.1.call-start = ((), (), s32[]{:S(2)}) async-start(), calls=%async_computation.2 | async-start | bytes 4210688 | tf_op jit(solution)/shard_map/all_gather | solution.py:124
  370.1 408.2 %all-reduce.11.cloned.1.call-start = ((), (), s32[]{:S(2)}) async-start(), calls=%async_computation.5 | async-start | bytes 16777216
  370.1 125.2 %copy-start.3 = (s32[2]{0:T(128)S(1)}, s32[2]{0:T(128)}, u32[]{:S(2)}) copy-start(s32[2]{0:T(128)} %param.15) | copy-start | bytes 28
Sparse Core Ops, SparseCore 0:
  41.9 106.1 all-reduce.6
  150.0 42.8 all-gather.8
  194.9 40.6 all-gather.6
  259.9 108.0 all-reduce.8
  372.1 115.9 all-gather.10
  503.6 274.6 all-reduce.10
where the time goes:
time: 791 us; the launch traced here: 790 us
  waiting for transfers between devices  601 us (76%)
  blocking collectives  114 us (14%)
  matrix products  27.2 us (3%)
  local copies, waits for them, and re-layouts  17.2 us (2%)
  between operations  16.8 us (2%)
  other arithmetic  12.8 us (2%)
    unnamed x9, waiting for transfers between devices  407 us
    all_gather x1, waiting for transfers between devices, local(): everyone = lax.all_gather(embedding, ('dp', 'fsdp'), axis=0, tiled=True)  118 us
    psum x1, blocking collectives, local(): loss = lax.psum(jnp.sum(jnp.log(total) - target), ('dp', 'fsdp')) / texts  75.3 us
    all_gather x1, waiting for transfers between devices, local(): lax.all_gather(key_weight, 'fsdp', axis=0, tiled=True)  43.8 us
    all_gather x1, waiting for transfers between devices, local(): lax.all_gather(value_weight, 'fsdp', axis=0, tiled=True)  33 us
    all_gather x1, blocking collectives, local(): all_pooled = lax.all_gather(pooled, 'fsdp', axis=0, tiled=True)  22 us
    all_gather x1, blocking collectives, local(): all_mixed = lax.all_gather(mixed, 'fsdp', axis=0, tiled=True)  16.7 us
  transfers between devices with their start and end apart: 6, of which 6 were waited for; matrix products, arithmetic and copies ran while one was open for 2% of the time, Pallas kernels for 0%

commit v1 on v0

v1 whole, which is shorter than its diff:
```python
import functools
import math

import jax
import jax.numpy as jnp
import numpy as np
from jax import lax
from jax.experimental import pallas as pl
from jax.experimental.pallas import tpu as pltpu
from jax.sharding import PartitionSpec as P

QUERY_HEADS = 16
KEY_VALUE_HEADS = 4
HEAD_SIZE = 128
WIDTH = 4096
TOKENS = 512
TEXTS = 512
LEAST_LAST = 191
MOST_LAST = 319
SIDE = 4
ND = 16
NF = 16
COLS = WIDTH // NF

EPS = 1e-06
THETA = 1000000.0
TEMPER = 0.05

F32 = jnp.float32
BF16 = jnp.bfloat16


def rotary_tables():
    half = HEAD_SIZE // 2
    freq = (THETA ** (-np.arange(half, dtype=np.float64) * 2.0 / HEAD_SIZE)).astype(np.float32)
    angle = np.arange(TOKENS, dtype=np.float32)[:, None] * freq[None, :]
    cosine, sine = np.cos(angle), np.sin(angle)
    return (
        np.concatenate([cosine, cosine], axis=1).astype(np.float32),
        np.concatenate([-sine, sine], axis=1).astype(np.float32),
    )


def remote(src, dst, send_sem, recv_sem, device):
    return pltpu.make_async_remote_copy(
        src_ref=src,
        dst_ref=dst,
        send_sem=send_sem,
        recv_sem=recv_sem,
        device_id=device,
        device_id_type=pl.DeviceIdType.MESH,
    )


def wait_bytes(ref, sem):
    pltpu.make_async_copy(ref, ref, sem).wait()


class Place:
    def __init__(self):
        self.d = lax.axis_index("dp")
        self.f = lax.axis_index("fsdp")
        self.x, self.y = self.d // SIDE, self.d % SIDE
        self.z, self.c = self.f // 2, self.f % 2
        self.sibling = (self.d, self.f + 1 - 2 * self.c)

    def index(self, k1, k2):
        xx = lax.rem(self.x + k1 * (1 - self.c) + k2 * self.c, SIDE)
        yy = lax.rem(self.y + k1 * self.c + k2 * (1 - self.c), SIDE)
        return xx * SIDE + yy


class Gather:
    def __init__(self, place, source, piece, block, half, most, whole, seven, sems):
        self.p, self.source, self.piece = place, source, piece
        self.block, self.half, self.most, self.whole, self.seven = block, half, most, whole, seven
        self.s1_send, self.s1_sib, self.s1_recv, self.sends, self.sib_send, self.sib_recv, self.r1, self.r2 = sems
        self.own_half = place.f // (NF // 2)

    def start(self):
        p = self.p
        core = self.own_half
        dst = self.piece(p.f, p.d)

        def one(k, carry):
            z = lax.rem(p.z + k, NF // 2)
            remote(self.source, dst, self.s1_send, self.s1_recv, (p.d, z * 2 + core)).start()
            return carry

        lax.fori_loop(1, NF // 2, one, 0)

        @pl.when(p.c == core)
        def _():
            pltpu.make_async_copy(self.source, dst, self.s1_recv).start()

        @pl.when(p.c != core)
        def _():
            remote(self.source, dst, self.s1_sib, self.s1_recv, p.sibling).start()

    def to_second(self, k1):
        p = self.p
        ref = self.block(p.c, p.index(k1, 0))
        remote(ref, ref, self.sends, self.r2.at[k1, 0], (p.index(0, 1), p.f)).start()
        remote(ref, ref, self.sends, self.r2.at[k1, 1], (p.index(0, 3), p.f)).start()

    def to_sibling(self, k1, k2):
        ref = self.block(self.p.c, self.p.index(k1, k2))
        remote(ref, ref, self.sib_send, self.sib_recv, self.p.sibling).start()

    def own(self):
        p = self.p
        ref = self.block(p.c, p.d)
        wait_bytes(ref, self.s1_recv)
        remote(ref, ref, self.sends, self.r1.at[0], (p.index(1, 0), p.f)).start()
        remote(ref, ref, self.sends, self.r1.at[1], (p.index(3, 0), p.f)).start()
        self.to_second(0)
        self.to_sibling(0, 0)

    def first_near(self):
        p = self.p
        for side, k in ((0, 3), (1, 1)):
            e = p.index(k, 0)
            wait_bytes(self.block(p.c, e), self.r1.at[side])
            ref = self.half(p.c, e, side)
            remote(ref, ref, self.sends, self.r1.at[2 + side], (p.index(4 - k, 0), p.f)).start()
            self.to_second(k)
            self.to_sibling(k, 0)

    def first_far(self):
        p = self.p
        e = p.index(2, 0)
        for side in (0, 1):
            wait_bytes(self.half(p.c, e, side), self.r1.at[2 + side])
        self.to_second(2)
        self.to_sibling(2, 0)

    def second_near(self, k1s=(0, 3, 1, 2)):
        p = self.p
        for k1 in k1s:
            for side, k in ((0, 3), (1, 1)):
                e = p.index(k1, k)
                wait_bytes(self.block(p.c, e), self.r2.at[k1, side])
                ref = self.half(p.c, e, side)
                remote(ref, ref, self.sends, self.r2.at[k1, 2 + side], (p.index(0, 4 - k), p.f)).start()
                self.to_sibling(k1, k)

    def second_far(self):
        p = self.p
        for k1 in (0, 3, 1, 2):
            e = p.index(k1, 2)
            for side in (0, 1):
                wait_bytes(self.half(p.c, e, side), self.r2.at[k1, 2 + side])
            self.to_sibling(k1, 2)

    def finish(self):
        wait_bytes(self.whole(1 - self.p.c), self.sib_recv)

    def drain(self):
        p = self.p
        wait_bytes(self.seven, self.s1_send)

        @pl.when(p.c != self.own_half)
        def _():
            wait_bytes(self.source, self.s1_sib)

        wait_bytes(self.most(p.c), self.sends)
        wait_bytes(self.whole(p.c), self.sib_send)


def all_to_all(place, source, target, send_sem, recv_sem):
    p = place

    def one(k, carry):
        g = lax.rem(p.f + k, NF)
        remote(source(g), target(p.f), send_sem, recv_sem, (p.d, g)).start()
        return carry

    pltpu.make_async_copy(source(p.f), target(p.f), recv_sem).start()
    lax.fori_loop(1, NF, one, 0)


def mean_square(rows):
    return jnp.mean(rows * rows, axis=-1, keepdims=True)


def kernel(
    lengths, partner, stream_hbm, norm_gain, wq_hbm, wk_hbm, wv_hbm, wo_hbm, q_gain, k_gain, final_gain,
    cos_hbm, sin_hbm,
    grad_out, loss_out,
    stream, normed, wk, wv, everyone, wq, wo, cos_t, sin_t,
    pool_send, pool_recv, q_send, q_recv, mix_send, mix_recv, mix_f32,
    ab_send, ab_recv, c_send, c_recv, u_send, keys, values, sim,
    load_sem, pair_sem,
    k1s, k1b, k1r, ks, kbs, kbr, kr1, kr2,
    v1s, v1b, v1r, vs, vbs, vbr, vr1, vr2,
    u1s, u1b, u1r, us, ubs, ubr, ur1, ur2,
):
    p = Place()
    d, f = p.d, p.f
    rows_of = lambda g, n: pl.ds(pl.multiple_of(g * n, n), n)
    lanes_of = lambda g, n: pl.ds(pl.multiple_of(g * n, n), n)

    quarter = TOKENS // 4
    loads = [
        pltpu.make_async_copy(stream_hbm.at[pl.ds(i * quarter, quarter)], stream.at[pl.ds(i * quarter, quarter)], load_sem.at[i])
        for i in range(4)
    ]
    loads += [
        pltpu.make_async_copy(wq_hbm, wq, load_sem.at[4]),
        pltpu.make_async_copy(cos_hbm, cos_t, load_sem.at[5]),
        pltpu.make_async_copy(sin_hbm, sin_t, load_sem.at[6]),
    ]
    for load in loads:
        load.start()

    barrier = pltpu.get_barrier_semaphore()

    def greet(k, carry):
        pl.semaphore_signal(barrier, inc=1, device_id=(d, lax.rem(f + k, NF)), device_id_type=pl.DeviceIdType.MESH)
        pl.semaphore_signal(barrier, inc=1, device_id=(lax.rem(d + k, ND), f), device_id_type=pl.DeviceIdType.MESH)
        return carry

    lax.fori_loop(1, NF, greet, 0)
    pl.semaphore_wait(barrier, NF - 1 + ND - 1)

    def weight_gather(hbm, w, sems):
        return Gather(
            p,
            hbm.at[rows_of(d, 16)],
            lambda g, e: w.at[g, e],
            lambda c, e: w.at[pl.ds(c * 8, 8), e],
            lambda c, e, s: w.at[pl.ds(c * 8 + s * 4, 4), e],
            lambda c: w.at[pl.ds(c * 8, 8), pl.ds(0, 15)],
            lambda c: w.at[pl.ds(c * 8, 8)],
            w.at[0, pl.ds(0, 7)],
            sems,
        )

    k_gather = weight_gather(wk_hbm, wk, (k1s, k1b, k1r, ks, kbs, kbr, kr1, kr2))
    v_gather = weight_gather(wv_hbm, wv, (v1s, v1b, v1r, vs, vbs, vbr, vr1, vr2))
    u_gather = Gather(
        p,
        u_send,
        lambda g, e: everyone.at[e, :, lanes_of(g, COLS)],
        lambda c, e: everyone.at[e, :, lanes_of(c, WIDTH // 2)],
        lambda c, e, s: everyone.at[e, :, lanes_of(c * 2 + s, WIDTH // 4)],
        lambda c: everyone.at[pl.ds(0, 15), :, lanes_of(c, WIDTH // 2)],
        lambda c: everyone.at[:, :, lanes_of(c, WIDTH // 2)],
        everyone.at[0, :, pl.ds(0, 7 * COLS)],
        (u1s, u1b, u1r, us, ubs, ubr, ur1, ur2),
    )

    k_gather.start()

    for load in loads[:4]:
        load.wait()
    last = lengths[0, 0] - 1
    gain = norm_gain[...].astype(F32)
    for t in range(2):
        if t == 0:
            row = jnp.zeros((16, WIDTH), F32)
            for start in range(LEAST_LAST // 16 * 16, MOST_LAST + 1, 16):
                here = lax.broadcasted_iota(jnp.int32, (16, WIDTH), 0) == last - start
                row += jnp.where(here, stream[pl.ds(start, 16), :].astype(F32), 0.0)
            row = jnp.sum(row, axis=0, keepdims=True)
        else:
            row = stream[pl.ds(TOKENS - 16, 16), :].astype(F32)[15:16]
        norm_row = (row * lax.rsqrt(mean_square(row) + EPS) * gain).astype(BF16).astype(F32)
        for g in range(NF):
            for h in range(2):
                lane = g * COLS + h * 128
                pool_send[pl.ds(g * 8 + t * 2 + h, 1), :] = norm_row[:, lane : lane + 128]
                pool_send[pl.ds(g * 8 + 4 + t * 2 + h, 1), :] = row[:, lane : lane + 128]
    all_to_all(
        p, lambda g: pool_send.at[rows_of(g, 8)], lambda g: pool_recv.at[rows_of(g, 8)], pair_sem.at[0], pair_sem.at[1]
    )
    v_gather.start()
    k_gather.own()

    def norm_rows(i, carry):
        rows = pl.ds(pl.multiple_of(i * 32, 32), 32)
        block = stream[rows, :].astype(F32)
        normed[rows, :] = (block * lax.rsqrt(mean_square(block) + EPS) * gain).astype(BF16)
        return carry

    lax.fori_loop(0, TOKENS // 32, norm_rows, 0)

    for load in loads[4:]:
        load.wait()
    wait_bytes(pool_recv, pair_sem.at[1])

    def pooled_block(first):
        return jnp.concatenate(
            [
                jnp.concatenate([pool_recv[pl.ds(first + t * 2 + h, NF, stride=8), :] for h in range(2)], axis=1)
                for t in range(2)
            ],
            axis=0,
        )

    shares = jnp.dot(pooled_block(0).astype(BF16), wq[...], preferred_element_type=F32)
    for t in range(2):
        for h in range(QUERY_HEADS):
            q_send[pl.ds(t * 16 + h, NF, stride=32), :] = shares[t * 16 : t * 16 + 16, h * 128 : h * 128 + 128]
    all_to_all(
        p, lambda g: q_send.at[rows_of(g, 32)], lambda g: q_recv.at[rows_of(g, 32)], pair_sem.at[2], pair_sem.at[3]
    )

    k_gather.first_near()
    k_gather.first_far()
    v_gather.own()
    all_to_all(p, lambda g: wo_hbm.at[:, lanes_of(g, COLS)], lambda g: wo.at[g], pair_sem.at[4], pair_sem.at[5])

    wait_bytes(q_recv, pair_sem.at[3])
    query = q_recv[pl.ds(0, 32), :]
    for g in range(1, NF):
        query += q_recv[pl.ds(g * 32, 32), :]
    query = query * lax.rsqrt(mean_square(query) + EPS) * q_gain[...].astype(F32)
    row32 = lax.broadcasted_iota(jnp.int32, (32, 128), 0)

    def pooled_angle(table):
        start = LEAST_LAST // 8 * 8
        rows = table[pl.ds(start, MOST_LAST + 1 - start), :]
        here = lax.broadcasted_iota(jnp.int32, rows.shape, 0) == last - start
        first = jnp.sum(jnp.where(here, rows, 0.0), axis=0, keepdims=True)
        return jnp.where(row32 < 16, first, table[pl.ds(TOKENS - 1, 1), :])

    query = query * pooled_angle(cos_t) + pltpu.roll(query, 64, 1) * pooled_angle(sin_t)
    group = row32 % 16 // 4
    q_block = jnp.concatenate(
        [jnp.where(group == g, query, 0.0) for g in range(KEY_VALUE_HEADS)], axis=1
    ).astype(BF16)

    k_gather.second_near()
    v_gather.first_near()
    v_gather.first_far()
    k_gather.second_far()
    k_gather.finish()

    key_gain = k_gain[...].astype(F32)

    def key_rows(i, carry):
        rows = pl.ds(pl.multiple_of(i * 128, 128), 128)
        product = jnp.dot(normed[rows, :], wk[...].reshape(WIDTH, 512), preferred_element_type=F32)
        for g in range(KEY_VALUE_HEADS):
            one = product[:, g * 128 : g * 128 + 128]
            one = one * lax.rsqrt(mean_square(one) + EPS) * key_gain
            one = one * cos_t[rows, :] + pltpu.roll(one, 64, 1) * sin_t[rows, :]
            keys[rows, g * 128 : g * 128 + 128] = one.astype(BF16)
        return carry

    lax.fori_loop(0, TOKENS // 128, key_rows, 0)
    scores = lax.dot_general(q_block, keys[...], (((1,), (1,)), ((), ())), preferred_element_type=F32)
    scores = scores * (1.0 / math.sqrt(HEAD_SIZE))
    token = lax.broadcasted_iota(jnp.int32, scores.shape, 1)
    first_text = lax.broadcasted_iota(jnp.int32, scores.shape, 0) < 16
    inside = (token < lengths[0, 0]) == first_text
    weights = jnp.where(inside, jnp.exp(scores), 0.0)
    probs = (weights / jnp.sum(weights, axis=1, keepdims=True)).astype(BF16)

    v_gather.second_near()
    v_gather.second_far()
    v_gather.finish()

    def value_rows(i, carry):
        rows = pl.ds(pl.multiple_of(i * 128, 128), 128)
        values[rows, :] = jnp.dot(
            normed[rows, :], wv[...].reshape(WIDTH, 512), preferred_element_type=F32
        ).astype(BF16)
        return carry

    lax.fori_loop(0, TOKENS // 128, value_rows, 0)
    all_mixed = jnp.dot(probs, values[...], preferred_element_type=F32)
    mixed = jnp.zeros((32, 128), F32)
    for g in range(KEY_VALUE_HEADS):
        mixed += jnp.where(group == g, all_mixed[:, g * 128 : g * 128 + 128], 0.0)
    mix_send[...] = mixed.astype(BF16)
    all_to_all(p, lambda g: mix_send, lambda g: mix_recv.at[g], pair_sem.at[6], pair_sem.at[7])
    wait_bytes(wo, pair_sem.at[5])
    wait_bytes(mix_recv, pair_sem.at[7])

    mix_f32[...] = mix_recv[...].astype(F32).reshape(NF * 32, 128)
    wide = jnp.concatenate(
        [
            jnp.concatenate([mix_f32[pl.ds(t * 16 + h, NF, stride=32), :] for h in range(QUERY_HEADS)], axis=1)
            for t in range(2)
        ],
        axis=0,
    ).astype(BF16)
    state = pooled_block(4) + jnp.dot(wide, wo[...].reshape(2048, COLS), preferred_element_type=F32)
    gained = state * final_gain[:, lanes_of(f, COLS)].astype(F32)
    u_send[...] = gained.astype(BF16)
    u_gather.start()

    offset = d % 4 * 32
    row = lax.broadcasted_iota(jnp.int32, (32, 128), 0)
    lane = lax.broadcasted_iota(jnp.int32, (32, 128), 1)
    diagonal = lane == row + offset
    as_lanes = lambda column: jnp.sum(jnp.where(diagonal, column, 0.0), axis=0, keepdims=True)
    square = as_lanes(jnp.sum(state * state, axis=1, keepdims=True))
    gained_square = as_lanes(jnp.sum(gained * gained, axis=1, keepdims=True))
    lane1 = lax.broadcasted_iota(jnp.int32, (1, 128), 1)
    own = [partner[0, 0], partner[0, 1]]
    partners = jnp.where(lane1 == offset + f, own[0], 0) + jnp.where(lane1 == offset + 16 + f, own[1], 0)
    row8 = lax.broadcasted_iota(jnp.int32, (8, 128), 0)
    pack = lambda parts: functools.reduce(
        lambda total, item: jnp.where(row8 == item[0], item[1], total), enumerate(parts), jnp.zeros((8, 128), F32)
    )
    ab_send[...] = pack([square, gained_square, partners.astype(F32)])
    all_to_all(p, lambda g: ab_send, lambda g: ab_recv.at[rows_of(g, 8)], pair_sem.at[8], pair_sem.at[9])
    u_gather.own()

    wait_bytes(ab_recv, pair_sem.at[9])
    sums = ab_recv[pl.ds(0, 8), :]
    for g in range(1, NF):
        sums += ab_recv[pl.ds(g * 8, 8), :]
    inverse = lax.rsqrt(sums[0:1] / WIDTH + EPS)
    factor = inverse * lax.rsqrt(inverse * inverse * sums[1:2] + EPS)
    factor = jnp.where((lane1 >= offset) & (lane1 < offset + 32), factor, 0.0)
    c_send[...] = pack([factor, sums[2:3]])

    def send_factor(k, carry):
        e = lax.rem(d + k, ND)
        remote(c_send, c_recv.at[rows_of(d, 8)], pair_sem.at[10], pair_sem.at[11], (e, f)).start()
        return carry

    pltpu.make_async_copy(c_send, c_recv.at[rows_of(d, 8)], pair_sem.at[11]).start()
    lax.fori_loop(1, ND, send_factor, 0)

    u_gather.first_near()
    u_gather.first_far()
    u_gather.second_near()
    u_gather.second_far()
    wait_bytes(c_recv, pair_sem.at[11])
    folded = []
    for q in range(4):
        folded.append(sum(c_recv[pl.ds((q * 4 + i) * 8, 8), :] for i in range(1, 4)) + c_recv[pl.ds(q * 32, 8), :])
    factor_row = jnp.concatenate([block[0:1] for block in folded], axis=1)
    partner_row = jnp.concatenate([block[1:2] for block in folded], axis=1).astype(jnp.int32)
    square_row = lax.broadcasted_iota(jnp.int32, (128, 128), 0)
    square_lane = lax.broadcasted_iota(jnp.int32, (128, 128), 1)
    factor_column = [
        jnp.sum(jnp.where(square_row == square_lane, block[0:1], 0.0), axis=1, keepdims=True) for block in folded
    ]
    u_gather.finish()

    name_of = lambda j: j // 32 * 32 + j % 16 * 2 + j % 32 // 16
    total = jnp.zeros((1, TEXTS), F32)
    target = jnp.zeros((1, TEXTS), F32)
    for i in range(4):
        rows = pl.ds(i * 128, 128)
        block = lax.dot_general(
            everyone[pl.ds(i * 4, 4)].reshape(128, WIDTH),
            everyone[...].reshape(TEXTS, WIDTH),
            (((1,), (1,)), ((), ())),
            preferred_element_type=F32,
        )
        block = block * (factor_column[i] * (1.0 / TEMPER)) * factor_row
        sim[rows, :] = block
        i_index = lax.broadcasted_iota(jnp.int32, block.shape, 0) + i * 128
        j_index = lax.broadcasted_iota(jnp.int32, block.shape, 1)
        hit = name_of(i_index) == partner_row
        total += jnp.sum(jnp.where((i_index != j_index) | hit, jnp.exp(block), 0.0), axis=0, keepdims=True)
        target += jnp.sum(jnp.where(hit, block, 0.0), axis=0, keepdims=True)
    loss_out[...] = jnp.sum(jnp.log(total) - target, axis=1, keepdims=True) * (1.0 / TEXTS)

    j_index = lax.broadcasted_iota(jnp.int32, (1, TEXTS), 1)
    names = name_of(j_index)
    coefficient = []
    for t in range(2):
        place = d * 32 + t * 16 + f
        name = (d * NF + f) * 2 + t
        exps = jnp.exp(sim[pl.ds(place, 1), :])
        own_total = jnp.sum(jnp.where(j_index == place, total, 0.0), axis=1, keepdims=True)
        other = j_index != place
        hit = names == own[t]
        back = partner_row == name
        pull = jnp.where(other | hit, exps, 0.0) / own_total - hit.astype(F32)
        pulled = jnp.where(other | back, exps, 0.0) / total - back.astype(F32)
        coefficient.append((pull.astype(BF16).astype(F32) + pulled.astype(BF16).astype(F32)) * factor_row)
    high = [item.astype(BF16).astype(F32) for item in coefficient]
    low = [item - part for item, part in zip(coefficient, high)]
    row16 = lax.broadcasted_iota(jnp.int32, (16, TEXTS), 0)
    stack = jnp.zeros((16, TEXTS), F32)
    for n, item in enumerate(high + low):
        stack = jnp.where(row16 == n, item, stack)
    stack = stack.astype(BF16)
    for n in range(4):
        part = jnp.dot(
            stack,
            everyone[:, :, n * 1024 : n * 1024 + 1024].reshape(TEXTS, 1024),
            preferred_element_type=F32,
        )
        grad_out[:, n * 1024 : n * 1024 + 1024] = (part[0:2] + part[2:4]) * (1.0 / TEMPER)

    for gather in (k_gather, v_gather, u_gather):
        gather.drain()
    wait_bytes(pool_send.at[pl.ds(0, 15 * 8)], pair_sem.at[0])
    wait_bytes(q_send.at[pl.ds(0, 15 * 32)], pair_sem.at[2])
    wait_bytes(wo.at[pl.ds(0, 15)], pair_sem.at[4])
    wait_bytes(mix_recv.at[pl.ds(0, 15)], pair_sem.at[6])
    wait_bytes(ab_recv.at[pl.ds(0, 15 * 8)], pair_sem.at[8])
    wait_bytes(c_recv.at[pl.ds(0, 15 * 8)], pair_sem.at[10])


def local(
    stream, lengths, partner, norm_gain, w_query, key_weight, value_weight, w_out, q_gain, key_norm_gain, final_gain
):
    cos_table, sin_table = rotary_tables()
    vmem = pl.BlockSpec(memory_space=pltpu.VMEM)
    smem = pl.BlockSpec(memory_space=pltpu.SMEM)
    hbm = pl.BlockSpec(memory_space=pltpu.HBM)
    dma = pltpu.SemaphoreType.DMA
    gather_sems = [dma, dma, dma, dma, dma, dma, dma((4,)), dma((4, 4))]
    grad, loss = pl.pallas_call(
        kernel,
        out_shape=(
            jax.ShapeDtypeStruct((2, WIDTH), F32),
            jax.ShapeDtypeStruct((1, 1), F32),
        ),
        in_specs=[smem, smem, hbm, vmem, hbm, hbm, hbm, hbm, vmem, vmem, vmem, hbm, hbm],
        out_specs=(vmem, vmem),
        scratch_shapes=[
            pltpu.VMEM((TOKENS, WIDTH), BF16),
            pltpu.VMEM((TOKENS, WIDTH), BF16),
            pltpu.VMEM((NF, ND, 16, 512), BF16),
            pltpu.VMEM((NF, ND, 16, 512), BF16),
            pltpu.VMEM((ND, 32, WIDTH), BF16),
            pltpu.VMEM((COLS, 2048), BF16),
            pltpu.VMEM((NF, 128, COLS), BF16),
            pltpu.VMEM((TOKENS, HEAD_SIZE), F32),
            pltpu.VMEM((TOKENS, HEAD_SIZE), F32),
            pltpu.VMEM((NF * 8, 128), F32),
            pltpu.VMEM((NF * 8, 128), F32),
            pltpu.VMEM((NF * 32, 128), F32),
            pltpu.VMEM((NF * 32, 128), F32),
            pltpu.VMEM((32, 128), BF16),
            pltpu.VMEM((NF, 32, 128), BF16),
            pltpu.VMEM((NF * 32, 128), F32),
            pltpu.VMEM((8, 128), F32),
            pltpu.VMEM((NF * 8, 128), F32),
            pltpu.VMEM((8, 128), F32),
            pltpu.VMEM((ND * 8, 128), F32),
            pltpu.VMEM((32, COLS), BF16),
            pltpu.VMEM((TOKENS, 512), BF16),
            pltpu.VMEM((TOKENS, 512), BF16),
            pltpu.VMEM((TEXTS, TEXTS), F32),
            dma((7,)),
            dma((12,)),
        ]
        + gather_sems * 3,
        compiler_params=pltpu.CompilerParams(
            collective_id=0, has_side_effects=True, vmem_limit_bytes=60 * 1024 * 1024
        ),
    )(
        lengths,
        partner.reshape(1, 2),
        stream,
        norm_gain.reshape(1, WIDTH),
        w_query,
        key_weight,
        value_weight,
        w_out,
        q_gain.reshape(1, HEAD_SIZE),
        key_norm_gain.reshape(1, HEAD_SIZE),
        final_gain.reshape(1, WIDTH),
        jnp.asarray(cos_table),
        jnp.asarray(sin_table),
    )
    return (grad, loss.reshape(()))


def solution(mesh):
    return jax.shard_map(
        local,
        mesh=mesh,
        in_specs=(
            P(("dp", "fsdp"), None),
            P(("dp", "fsdp"), None),
            P(("dp", "fsdp")),
            P(),
            P("fsdp", None),
            P("fsdp", None),
            P("fsdp", None),
            P("fsdp", None),
            P(),
            P(),
            P(),
        ),
        out_specs=(P(("dp", "fsdp"), None), P()),
        check_vma=False,
    )
```

time: 791 us -> 101 us (0.13)
  waiting for transfers between devices: 601 us -> 0 us
  blocking collectives: 114 us -> 0 us
  Pallas kernels: 0 us -> 94.4 us
  matrix products: 27.2 us -> 0 us
  between operations: 16.8 us -> 2.38 us
  local copies, waits for them, and re-layouts: 17.2 us -> 3.99 us
  other arithmetic: 12.8 us -> 0 us
    unnamed x9 -> x0, waiting for transfers between devices: 407 us -> none
    all_gather x3 -> x0, waiting for transfers between devices: 195 us -> none  [the longest x1 118 us: local(): everyone = lax.all_gather(embedding, ('dp', 'fsdp'), axis=0, tiled=True)]
    pallas_call x0 -> x1, Pallas kernels: none -> 94.4 us  [local(): pl.pallas_call(kernel, out_shape=(jax.ShapeDtypeStruct((2, WIDTH), F32),...]
    psum x1 -> x0, blocking collectives: 75.3 us -> none  [local(): loss = lax.psum(jnp.sum(jnp.log(total) - target), ('dp', 'fsdp')) / texts]
    all_gather x2 -> x0, blocking collectives: 38.8 us -> none  [the longest x1 22 us: local(): all_pooled = lax.all_gather(pooled, 'fsdp', axis=0, tiled=True)]
    dot_general x9 -> x0, matrix products: 27.2 us -> none  [the longest x1 6.9 us: local(): jnp.dot(columns, lax.all_gather(key_weight, 'fsdp', axis=0, tiled=True),...]
  transfers between devices with their start and end apart: 6 -> 0, of which waited for: 6 -> 0; matrix products, arithmetic and copies ran while one was open for 2% -> 0% of each run, Pallas kernels for 0% -> 0%
where the time goes in v1:
time: 101 us
  Pallas kernels  94.4 us (93%)
  local copies, waits for them, and re-layouts  3.99 us (4%)
  between operations  2.38 us (2%)
    pallas_call x1, Pallas kernels, local(): pl.pallas_call(kernel, out_shape=(jax.ShapeDtypeStruct((2, WIDTH), F32),...  94.4 us

profile of v1, /device:TPU:1, one launch (start us, length us, event | category | flops | bytes accessed | tf_op | source)
XLA Modules:
  0.0 100.8 jit_solution(10676288755958940440)
XLA Ops:
  0.6 1.3 %reshape.23.norm_gain = bf16[1,4096]{1,0:T(2,128)(2,1)} reshape(bf16[4096]{0:T(1024)(128)(2,1)} %param.16) | data formatting | bytes 16384 | tf_op jit(solution)/shard_map/reshape | solution.py:559
  1.9 1.3 %reshape.26.final_gain = bf16[1,4096]{1,0:T(2,128)(2,1)} reshape(bf16[4096]{0:T(1024)(128)(2,1)} %param.23) | data formatting | bytes 16384 | tf_op jit(solution)/shard_map/reshape | solution.py:566
  3.2 94.4 %shard_map.140 = (f32[2,4096]{1,0:T(2,128)}, f32[1,1]{1,0:T(1,128)}) custom-call(s32[1,2]{1,0:T(1,128)} %lengths.1, s32[1,2]{1,0:T(1,128)} %bitcast.4, bf16[512,4096]{1,0:T(8,128)(2,1)} %stream_hbm.1, bf16[1,4096]{1,0:T(2,128)(2,1)} %reshape.23.norm_gain, bf16[256,2048]{1,0:T(8,128)(2,1)} %wq_hbm.1, bf16[256,512]{1,0:T(8,128)(2,1)} %wk_hbm.1, ...), custom_call_target="tpu_custom_call" | custom-call | tf_op jit(solution)/shard_map/pallas_call | solution.py:515
  97.7 1.4 %copy.17 = f32[2,4096]{1,0:T(2,128)} copy(f32[2,4096]{1,0:T(2,128)} %get-tuple-element.8) | data formatting | bytes 65536

commit v2 on v1

--- a/solution.py
+++ b/solution.py
@@ -71,6 +71,8 @@
 
 
 class Gather:
+    straight = (2,)
+
     def __init__(self, place, source, piece, block, half, most, whole, seven, sems):
         self.p, self.source, self.piece = place, source, piece
         self.block, self.half, self.most, self.whole, self.seven = block, half, most, whole, seven
@@ -102,6 +104,8 @@
         ref = self.block(p.c, p.index(k1, 0))
         remote(ref, ref, self.sends, self.r2.at[k1, 0], (p.index(0, 1), p.f)).start()
         remote(ref, ref, self.sends, self.r2.at[k1, 1], (p.index(0, 3), p.f)).start()
+        if k1 in self.straight:
+            remote(ref, ref, self.sends, self.r2.at[k1, 2], (p.index(0, 2), p.f)).start()
 
     def to_sibling(self, k1, k2):
         ref = self.block(self.p.c, self.p.index(k1, k2))
@@ -113,6 +117,7 @@
         wait_bytes(ref, self.s1_recv)
         remote(ref, ref, self.sends, self.r1.at[0], (p.index(1, 0), p.f)).start()
         remote(ref, ref, self.sends, self.r1.at[1], (p.index(3, 0), p.f)).start()
+        remote(ref, ref, self.sends, self.r1.at[2], (p.index(2, 0), p.f)).start()
         self.to_second(0)
         self.to_sibling(0, 0)
 
@@ -121,16 +126,13 @@
         for side, k in ((0, 3), (1, 1)):
             e = p.index(k, 0)
             wait_bytes(self.block(p.c, e), self.r1.at[side])
-            ref = self.half(p.c, e, side)
-            remote(ref, ref, self.sends, self.r1.at[2 + side], (p.index(4 - k, 0), p.f)).start()
             self.to_second(k)
             self.to_sibling(k, 0)
 
     def first_far(self):
         p = self.p
         e = p.index(2, 0)
-        for side in (0, 1):
-            wait_bytes(self.half(p.c, e, side), self.r1.at[2 + side])
+        wait_bytes(self.block(p.c, e), self.r1.at[2])
         self.to_second(2)
         self.to_sibling(2, 0)
 
@@ -140,16 +142,20 @@
             for side, k in ((0, 3), (1, 1)):
                 e = p.index(k1, k)
                 wait_bytes(self.block(p.c, e), self.r2.at[k1, side])
-                ref = self.half(p.c, e, side)
-                remote(ref, ref, self.sends, self.r2.at[k1, 2 + side], (p.index(0, 4 - k), p.f)).start()
+                if k1 not in self.straight:
+                    ref = self.half(p.c, e, side)
+                    remote(ref, ref, self.sends, self.r2.at[k1, 2 + side], (p.index(0, 4 - k), p.f)).start()
                 self.to_sibling(k1, k)
 
     def second_far(self):
         p = self.p
         for k1 in (0, 3, 1, 2):
             e = p.index(k1, 2)
-            for side in (0, 1):
-                wait_bytes(self.half(p.c, e, side), self.r2.at[k1, 2 + side])
+            if k1 in self.straight:
+                wait_bytes(self.block(p.c, e), self.r2.at[k1, 2])
+            else:
+                for side in (0, 1):
+                    wait_bytes(self.half(p.c, e, side), self.r2.at[k1, 2 + side])
             self.to_sibling(k1, 2)
 
     def finish(self):
@@ -255,7 +261,7 @@
     for load in loads[:4]:
         load.wait()
     last = lengths[0, 0] - 1
-    gain = norm_gain[...].astype(F32)
+    gain = norm_gain[...].astype(F32).reshape(1, WIDTH)
     for t in range(2):
         if t == 0:
             row = jnp.zeros((16, WIDTH), F32)
@@ -309,7 +315,17 @@
     k_gather.first_near()
     k_gather.first_far()
     v_gather.own()
-    all_to_all(p, lambda g: wo_hbm.at[:, lanes_of(g, COLS)], lambda g: wo.at[g], pair_sem.at[4], pair_sem.at[5])
+    def wo_rows(core):
+        return pl.ds(pl.multiple_of((p.x * (1 - core) + p.y * core) * 32, 32), 32)
+
+    def send_wo(k, carry):
+        g = lax.rem(f + k, NF)
+        rows = wo_rows(g % 2)
+        remote(wo_hbm.at[rows, lanes_of(g, COLS)], wo.at[f, rows], pair_sem.at[4], pair_sem.at[5], (d, g)).start()
+        return carry
+
+    pltpu.make_async_copy(wo_hbm.at[wo_rows(p.c), lanes_of(f, COLS)], wo.at[f, wo_rows(p.c)], pair_sem.at[5]).start()
+    lax.fori_loop(1, NF, send_wo, 0)
 
     wait_bytes(q_recv, pair_sem.at[3])
     query = q_recv[pl.ds(0, 32), :]
@@ -335,15 +351,32 @@
     v_gather.first_near()
     v_gather.first_far()
     k_gather.second_far()
+
+    key_gain = k_gain[...].astype(F32)
+
+    def half_product(w, core, rows):
+        return jnp.dot(
+            normed[rows, lanes_of(core, WIDTH // 2)],
+            w[pl.ds(core * 8, 8)].reshape(WIDTH // 2, 512),
+            preferred_element_type=F32,
+        )
+
+    def first_half(w):
+        for i in range(2):
+            rows = pl.ds(i * 256, 256)
+            sim[rows, :] = half_product(w, p.c, rows)
+
+    first_half(wk)
     k_gather.finish()
-
-    key_gain = k_gain[...].astype(F32)
+    for i in range(2):
+        rows = pl.ds(i * 256, 256)
+        sim[rows, :] += half_product(wk, 1 - p.c, rows)
+    v_gather.second_near((0,))
 
     def key_rows(i, carry):
         rows = pl.ds(pl.multiple_of(i * 128, 128), 128)
-        product = jnp.dot(normed[rows, :], wk[...].reshape(WIDTH, 512), preferred_element_type=F32)
         for g in range(KEY_VALUE_HEADS):
-            one = product[:, g * 128 : g * 128 + 128]
+            one = sim[rows, g * 128 : g * 128 + 128]
             one = one * lax.rsqrt(mean_square(one) + EPS) * key_gain
             one = one * cos_t[rows, :] + pltpu.roll(one, 64, 1) * sin_t[rows, :]
             keys[rows, g * 128 : g * 128 + 128] = one.astype(BF16)
@@ -358,25 +391,25 @@
     weights = jnp.where(inside, jnp.exp(scores), 0.0)
     probs = (weights / jnp.sum(weights, axis=1, keepdims=True)).astype(BF16)
 
-    v_gather.second_near()
+    v_gather.second_near((3, 1, 2))
     v_gather.second_far()
+    own_wo = wo.at[:, wo_rows(p.c)]
+    wait_bytes(own_wo, pair_sem.at[5])
+    for k in (1, 3, 2):
+        remote(own_wo, own_wo, pair_sem.at[12], pair_sem.at[13], (p.index(k, 0), f)).start()
+
+    first_half(wv)
     v_gather.finish()
-
-    def value_rows(i, carry):
-        rows = pl.ds(pl.multiple_of(i * 128, 128), 128)
-        values[rows, :] = jnp.dot(
-            normed[rows, :], wv[...].reshape(WIDTH, 512), preferred_element_type=F32
-        ).astype(BF16)
-        return carry
-
-    lax.fori_loop(0, TOKENS // 128, value_rows, 0)
+    for i in range(2):
+        rows = pl.ds(i * 256, 256)
+        values[rows, :] = (sim[rows, :] + half_product(wv, 1 - p.c, rows)).astype(BF16)
     all_mixed = jnp.dot(probs, values[...], preferred_element_type=F32)
     mixed = jnp.zeros((32, 128), F32)
     for g in range(KEY_VALUE_HEADS):
         mixed += jnp.where(group == g, all_mixed[:, g * 128 : g * 128 + 128], 0.0)
     mix_send[...] = mixed.astype(BF16)
     all_to_all(p, lambda g: mix_send, lambda g: mix_recv.at[g], pair_sem.at[6], pair_sem.at[7])
-    wait_bytes(wo, pair_sem.at[5])
+    wait_bytes(wo.at[pl.ds(0, 12)], pair_sem.at[13])
     wait_bytes(mix_recv, pair_sem.at[7])
 
     mix_f32[...] = mix_recv[...].astype(F32).reshape(NF * 32, 128)
@@ -388,7 +421,7 @@
         axis=0,
     ).astype(BF16)
     state = pooled_block(4) + jnp.dot(wide, wo[...].reshape(2048, COLS), preferred_element_type=F32)
-    gained = state * final_gain[:, lanes_of(f, COLS)].astype(F32)
+    gained = state * final_gain[lanes_of(f, COLS)].astype(F32).reshape(1, COLS)
     u_send[...] = gained.astype(BF16)
     u_gather.start()
 
@@ -442,22 +475,28 @@
     factor_column = [
         jnp.sum(jnp.where(square_row == square_lane, block[0:1], 0.0), axis=1, keepdims=True) for block in folded
     ]
+
+    def half_scores(core, i):
+        return lax.dot_general(
+            everyone[pl.ds(i * 8, 8), :, lanes_of(core, WIDTH // 2)].reshape(256, WIDTH // 2),
+            everyone[:, :, lanes_of(core, WIDTH // 2)].reshape(TEXTS, WIDTH // 2),
+            (((1,), (1,)), ((), ())),
+            preferred_element_type=F32,
+        )
+
+    for i in range(2):
+        sim[pl.ds(i * 256, 256), :] = half_scores(p.c, i)
     u_gather.finish()
-
     name_of = lambda j: j // 32 * 32 + j % 16 * 2 + j % 32 // 16
     total = jnp.zeros((1, TEXTS), F32)
     target = jnp.zeros((1, TEXTS), F32)
-    for i in range(4):
-        rows = pl.ds(i * 128, 128)
-        block = lax.dot_general(
-            everyone[pl.ds(i * 4, 4)].reshape(128, WIDTH),
-            everyone[...].reshape(TEXTS, WIDTH),
-            (((1,), (1,)), ((), ())),
-            preferred_element_type=F32,
-        )
-        block = block * (factor_column[i] * (1.0 / TEMPER)) * factor_row
+    for i in range(2):
+        rows = pl.ds(i * 256, 256)
+        block = sim[rows, :] + half_scores(1 - p.c, i)
+        column = jnp.concatenate(factor_column[i * 2 : i * 2 + 2], axis=0) * (1.0 / TEMPER)
+        block = block * column * factor_row
         sim[rows, :] = block
-        i_index = lax.broadcasted_iota(jnp.int32, block.shape, 0) + i * 128
+        i_index = lax.broadcasted_iota(jnp.int32, block.shape, 0) + i * 256
         j_index = lax.broadcasted_iota(jnp.int32, block.shape, 1)
         hit = name_of(i_index) == partner_row
         total += jnp.sum(jnp.where((i_index != j_index) | hit, jnp.exp(block), 0.0), axis=0, keepdims=True)
@@ -497,7 +536,8 @@
         gather.drain()
     wait_bytes(pool_send.at[pl.ds(0, 15 * 8)], pair_sem.at[0])
     wait_bytes(q_send.at[pl.ds(0, 15 * 32)], pair_sem.at[2])
-    wait_bytes(wo.at[pl.ds(0, 15)], pair_sem.at[4])
+    wait_bytes(wo.at[pl.ds(0, 15), pl.ds(0, 32)], pair_sem.at[4])
+    wait_bytes(wo.at[pl.ds(0, 12)], pair_sem.at[12])
     wait_bytes(mix_recv.at[pl.ds(0, 15)], pair_sem.at[6])
     wait_bytes(ab_recv.at[pl.ds(0, 15 * 8)], pair_sem.at[8])
     wait_bytes(c_recv.at[pl.ds(0, 15 * 8)], pair_sem.at[10])
@@ -546,7 +586,7 @@
             pltpu.VMEM((TOKENS, 512), BF16),
             pltpu.VMEM((TEXTS, TEXTS), F32),
             dma((7,)),
-            dma((12,)),
+            dma((14,)),
         ]
         + gather_sems * 3,
         compiler_params=pltpu.CompilerParams(
@@ -556,14 +596,14 @@
         lengths,
         partner.reshape(1, 2),
         stream,
-        norm_gain.reshape(1, WIDTH),
+        norm_gain,
         w_query,
         key_weight,
         value_weight,
         w_out,
         q_gain.reshape(1, HEAD_SIZE),
         key_norm_gain.reshape(1, HEAD_SIZE),
-        final_gain.reshape(1, WIDTH),
+        final_gain,
         jnp.asarray(cos_table),
         jnp.asarray(sin_table),
     )

time: 101 us -> 87.6 us (0.87)
  Pallas kernels: 94.4 us -> 83.6 us
  local copies, waits for them, and re-layouts: 3.99 us -> 1.38 us
    pallas_call x1, Pallas kernels: 94.4 us -> 83.6 us  [local(): pl.pallas_call(kernel, out_shape=(jax.ShapeDtypeStruct((2, WIDTH), F32),...]
    reshape x2 -> x0, local copies, waits for them, and re-layouts: 2.62 us -> none  [the longest x1 1.31 us: local(): norm_gain.reshape(1, WIDTH)]
where the time goes in v2:
time: 87.6 us; the launch traced here: 87.4 us
  Pallas kernels  83.6 us (95%)
  between operations  2.4 us (3%)
  local copies, waits for them, and re-layouts  1.38 us (2%)
    pallas_call x1, Pallas kernels, local(): pl.pallas_call(kernel, out_shape=(jax.ShapeDtypeStruct((2, WIDTH), F32),...  83.6 us

profile of v2, /device:TPU:1, one launch (start us, length us, event | category | flops | bytes accessed | tf_op | source)
XLA Modules:
  0.0 87.4 jit_solution(218924866799038918)
XLA Ops:
  0.6 83.6 %shard_map.140 = (f32[2,4096]{1,0:T(2,128)}, f32[1,1]{1,0:T(1,128)}) custom-call(s32[1,2]{1,0:T(1,128)} %lengths.1, s32[1,2]{1,0:T(1,128)} %bitcast.4, bf16[512,4096]{1,0:T(8,128)(2,1)} %stream_hbm.1, bf16[4096]{0:T(1024)(128)(2,1)} %norm_gain.1, bf16[256,2048]{1,0:T(8,128)(2,1)} %wq_hbm.1, bf16[256,512]{1,0:T(8,128)(2,1)} %wk_hbm.1, ...), custom_call_target="tpu_custom_call" | custom-call | tf_op jit(solution)/shard_map/pallas_call | solution.py:555
  84.2 1.4 %copy.17 = f32[2,4096]{1,0:T(2,128)} copy(f32[2,4096]{1,0:T(2,128)} %get-tuple-element.8) | data formatting | bytes 65536

commit v3 on v2

--- a/solution.py
+++ b/solution.py
@@ -17,6 +17,9 @@
 TEXTS = 512
 LEAST_LAST = 191
 MOST_LAST = 319
+K_STRAIGHT = (2,)
+V_STRAIGHT = ()
+U_STRAIGHT = ()
 SIDE = 4
 ND = 16
 NF = 16
@@ -71,106 +74,152 @@
 
 
 class Gather:
-    straight = (2,)
-
-    def __init__(self, place, source, piece, block, half, most, whole, seven, sems):
-        self.p, self.source, self.piece = place, source, piece
-        self.block, self.half, self.most, self.whole, self.seven = block, half, most, whole, seven
-        self.s1_send, self.s1_sib, self.s1_recv, self.sends, self.sib_send, self.sib_recv, self.r1, self.r2 = sems
-        self.own_half = place.f // (NF // 2)
-
-    def start(self):
-        p = self.p
-        core = self.own_half
-        dst = self.piece(p.f, p.d)
-
-        def one(k, carry):
-            z = lax.rem(p.z + k, NF // 2)
-            remote(self.source, dst, self.s1_send, self.s1_recv, (p.d, z * 2 + core)).start()
-            return carry
-
-        lax.fori_loop(1, NF // 2, one, 0)
-
-        @pl.when(p.c == core)
-        def _():
-            pltpu.make_async_copy(self.source, dst, self.s1_recv).start()
-
-        @pl.when(p.c != core)
-        def _():
-            remote(self.source, dst, self.s1_sib, self.s1_recv, p.sibling).start()
+    def __init__(self, place, block, half, most, straight, sems):
+        self.p, self.block, self.half, self.most, self.straight = place, block, half, most, straight
+        self.sends, self.sib_send, self.sib_recv, self.r1, self.r2 = sems
 
     def to_second(self, k1):
         p = self.p
-        ref = self.block(p.c, p.index(k1, 0))
+        ref = self.block(p.index(k1, 0))
         remote(ref, ref, self.sends, self.r2.at[k1, 0], (p.index(0, 1), p.f)).start()
         remote(ref, ref, self.sends, self.r2.at[k1, 1], (p.index(0, 3), p.f)).start()
         if k1 in self.straight:
             remote(ref, ref, self.sends, self.r2.at[k1, 2], (p.index(0, 2), p.f)).start()
 
-    def to_sibling(self, k1, k2):
-        ref = self.block(self.p.c, self.p.index(k1, k2))
+    def to_sibling(self, ref):
         remote(ref, ref, self.sib_send, self.sib_recv, self.p.sibling).start()
 
     def own(self):
         p = self.p
-        ref = self.block(p.c, p.d)
-        wait_bytes(ref, self.s1_recv)
+        ref = self.block(p.d)
         remote(ref, ref, self.sends, self.r1.at[0], (p.index(1, 0), p.f)).start()
         remote(ref, ref, self.sends, self.r1.at[1], (p.index(3, 0), p.f)).start()
         remote(ref, ref, self.sends, self.r1.at[2], (p.index(2, 0), p.f)).start()
         self.to_second(0)
-        self.to_sibling(0, 0)
+        self.to_sibling(ref)
 
     def first_near(self):
-        p = self.p
         for side, k in ((0, 3), (1, 1)):
-            e = p.index(k, 0)
-            wait_bytes(self.block(p.c, e), self.r1.at[side])
+            ref = self.block(self.p.index(k, 0))
+            wait_bytes(ref, self.r1.at[side])
             self.to_second(k)
-            self.to_sibling(k, 0)
+            self.to_sibling(ref)
 
     def first_far(self):
-        p = self.p
-        e = p.index(2, 0)
-        wait_bytes(self.block(p.c, e), self.r1.at[2])
+        ref = self.block(self.p.index(2, 0))
+        wait_bytes(ref, self.r1.at[2])
         self.to_second(2)
-        self.to_sibling(2, 0)
+        self.to_sibling(ref)
 
     def second_near(self, k1s=(0, 3, 1, 2)):
         p = self.p
         for k1 in k1s:
             for side, k in ((0, 3), (1, 1)):
                 e = p.index(k1, k)
-                wait_bytes(self.block(p.c, e), self.r2.at[k1, side])
+                wait_bytes(self.block(e), self.r2.at[k1, side])
                 if k1 not in self.straight:
-                    ref = self.half(p.c, e, side)
+                    ref = self.half(e, side)
                     remote(ref, ref, self.sends, self.r2.at[k1, 2 + side], (p.index(0, 4 - k), p.f)).start()
-                self.to_sibling(k1, k)
+                self.to_sibling(self.block(e))
 
     def second_far(self):
-        p = self.p
         for k1 in (0, 3, 1, 2):
-            e = p.index(k1, 2)
+            e = self.p.index(k1, 2)
             if k1 in self.straight:
-                wait_bytes(self.block(p.c, e), self.r2.at[k1, 2])
+                wait_bytes(self.block(e), self.r2.at[k1, 2])
             else:
                 for side in (0, 1):
-                    wait_bytes(self.half(p.c, e, side), self.r2.at[k1, 2 + side])
-            self.to_sibling(k1, 2)
+                    wait_bytes(self.half(e, side), self.r2.at[k1, 2 + side])
+            self.to_sibling(self.block(e))
+
+    def drain(self):
+        wait_bytes(self.most, self.sends)
+
+
+class WeightGather(Gather):
+    def __init__(self, place, hbm, w, straight, sems):
+        self.hbm, self.w = hbm, w
+        self.s1_send, self.s1_recv, self.near_send, self.near_recv, self.own_sem = sems[:5]
+        self.mine = w.at[place.c]
+        far = pl.ds(2, 5)
+        super().__init__(
+            place,
+            lambda e: w.at[place.c, far, e],
+            lambda e, s: w.at[place.c, far, e, :, pl.ds(s * 256, 256)],
+            w.at[place.c, far, pl.ds(0, 15)],
+            straight,
+            sems[5:],
+        )
+
+    def start(self):
+        p = self.p
+        source = self.hbm.at[p.d]
+        for k in (4, 3, 5, 2, 6):
+            z = lax.rem(p.z + 8 - k, 8)
+            remote(source, self.mine.at[k, p.d], self.s1_send, self.s1_recv, (p.d, z * 2 + p.c)).start()
+
+    def start_near(self):
+        p = self.p
+        for i, k in enumerate((1, 7)):
+            z = lax.rem(p.z + 8 - k, 8)
+            remote(self.hbm, self.mine.at[k], self.near_send, self.near_recv.at[i], (p.d, z * 2 + p.c)).start()
+        pltpu.make_async_copy(self.hbm, self.mine.at[0], self.own_sem).start()
+
+    def own(self):
+        wait_bytes(self.block(self.p.d), self.s1_recv)
+        super().own()
+
+    def own_shard(self):
+        wait_bytes(self.mine.at[0], self.own_sem)
+        self.to_sibling(self.mine.at[0])
+
+    def near(self):
+        for i, k in enumerate((1, 7)):
+            wait_bytes(self.mine.at[k], self.near_recv.at[i])
+            self.to_sibling(self.mine.at[k])
 
     def finish(self):
-        wait_bytes(self.whole(1 - self.p.c), self.sib_recv)
+        wait_bytes(self.w.at[1 - self.p.c], self.sib_recv)
 
     def drain(self):
+        super().drain()
+        wait_bytes(self.mine.at[pl.ds(2, 5), 0], self.s1_send)
+        wait_bytes(self.mine.at[pl.ds(1, 2)], self.near_send)
+        wait_bytes(self.mine, self.sib_send)
+
+
+class RowGather(Gather):
+    def __init__(self, place, source, held, straight, sems):
+        self.source, self.held = source, held
+        self.s1_send, self.s1_recv = sems[:2]
+        super().__init__(
+            place,
+            lambda e: held.at[place.c, e],
+            lambda e, s: held.at[place.c, e, :, pl.ds(s * 1024, 1024)],
+            held.at[place.c, pl.ds(0, 15)],
+            straight,
+            sems[2:],
+        )
+
+    def start(self):
         p = self.p
-        wait_bytes(self.seven, self.s1_send)
-
-        @pl.when(p.c != self.own_half)
-        def _():
-            wait_bytes(self.source, self.s1_sib)
-
-        wait_bytes(self.most(p.c), self.sends)
-        wait_bytes(self.whole(p.c), self.sib_send)
+        dst = self.held.at[p.c, p.d, :, pl.ds(pl.multiple_of(p.z * COLS, COLS), COLS)]
+        pltpu.make_async_copy(self.source, dst, self.s1_recv).start()
+        for k in (4, 3, 5, 2, 6, 1, 7):
+            z = lax.rem(p.z + k, 8)
+            remote(self.source, dst, self.s1_send, self.s1_recv, (p.d, z * 2 + p.c)).start()
+
+    def own(self):
+        wait_bytes(self.block(self.p.d), self.s1_recv)
+        super().own()
+
+    def finish(self):
+        wait_bytes(self.held.at[1 - self.p.c], self.sib_recv)
+
+    def drain(self):
+        super().drain()
+        wait_bytes(self.held.at[0, 0, :, pl.ds(0, 7 * COLS)], self.s1_send)
+        wait_bytes(self.held.at[self.p.c], self.sib_send)
 
 
 def all_to_all(place, source, target, send_sem, recv_sem):
@@ -193,13 +242,13 @@
     lengths, partner, stream_hbm, norm_gain, wq_hbm, wk_hbm, wv_hbm, wo_hbm, q_gain, k_gain, final_gain,
     cos_hbm, sin_hbm,
     grad_out, loss_out,
-    stream, normed, wk, wv, everyone, wq, wo, cos_t, sin_t,
+    stream, normed, gain_row, wk, wv, everyone, wq, wo, cos_t, sin_t,
     pool_send, pool_recv, q_send, q_recv, mix_send, mix_recv, mix_f32,
     ab_send, ab_recv, c_send, c_recv, u_send, keys, values, sim,
     load_sem, pair_sem,
-    k1s, k1b, k1r, ks, kbs, kbr, kr1, kr2,
-    v1s, v1b, v1r, vs, vbs, vbr, vr1, vr2,
-    u1s, u1b, u1r, us, ubs, ubr, ur1, ur2,
+    k0, k1, k2, k3, k4, k5, k6, k7, k8, k9,
+    v0, v1, v2, v3, v4, v5, v6, v7, v8, v9,
+    u0, u1, u2, u3, u4, u5, u6,
 ):
     p = Place()
     d, f = p.d, p.f
@@ -229,32 +278,9 @@
     lax.fori_loop(1, NF, greet, 0)
     pl.semaphore_wait(barrier, NF - 1 + ND - 1)
 
-    def weight_gather(hbm, w, sems):
-        return Gather(
-            p,
-            hbm.at[rows_of(d, 16)],
-            lambda g, e: w.at[g, e],
-            lambda c, e: w.at[pl.ds(c * 8, 8), e],
-            lambda c, e, s: w.at[pl.ds(c * 8 + s * 4, 4), e],
-            lambda c: w.at[pl.ds(c * 8, 8), pl.ds(0, 15)],
-            lambda c: w.at[pl.ds(c * 8, 8)],
-            w.at[0, pl.ds(0, 7)],
-            sems,
-        )
-
-    k_gather = weight_gather(wk_hbm, wk, (k1s, k1b, k1r, ks, kbs, kbr, kr1, kr2))
-    v_gather = weight_gather(wv_hbm, wv, (v1s, v1b, v1r, vs, vbs, vbr, vr1, vr2))
-    u_gather = Gather(
-        p,
-        u_send,
-        lambda g, e: everyone.at[e, :, lanes_of(g, COLS)],
-        lambda c, e: everyone.at[e, :, lanes_of(c, WIDTH // 2)],
-        lambda c, e, s: everyone.at[e, :, lanes_of(c * 2 + s, WIDTH // 4)],
-        lambda c: everyone.at[pl.ds(0, 15), :, lanes_of(c, WIDTH // 2)],
-        lambda c: everyone.at[:, :, lanes_of(c, WIDTH // 2)],
-        everyone.at[0, :, pl.ds(0, 7 * COLS)],
-        (u1s, u1b, u1r, us, ubs, ubr, ur1, ur2),
-    )
+    k_gather = WeightGather(p, wk_hbm, wk, K_STRAIGHT, (k0, k1, k2, k3, k4, k5, k6, k7, k8, k9))
+    v_gather = WeightGather(p, wv_hbm, wv, V_STRAIGHT, (v0, v1, v2, v3, v4, v5, v6, v7, v8, v9))
+    u_gather = RowGather(p, u_send, everyone, U_STRAIGHT, (u0, u1, u2, u3, u4, u5, u6))
 
     k_gather.start()
 
@@ -281,15 +307,23 @@
         p, lambda g: pool_send.at[rows_of(g, 8)], lambda g: pool_recv.at[rows_of(g, 8)], pair_sem.at[0], pair_sem.at[1]
     )
     v_gather.start()
-    k_gather.own()
+    k_gather.start_near()
+    gain_row[...] = gain
 
     def norm_rows(i, carry):
         rows = pl.ds(pl.multiple_of(i * 32, 32), 32)
         block = stream[rows, :].astype(F32)
-        normed[rows, :] = (block * lax.rsqrt(mean_square(block) + EPS) * gain).astype(BF16)
+        inverse = lax.rsqrt(mean_square(block) + EPS)
+        for k in range(8):
+            lanes = lanes_of(lax.rem(p.z + k, 8), 2 * COLS)
+            chunk = (stream[rows, lanes].astype(F32) * inverse * gain_row[:, lanes]).astype(BF16)
+            for core in range(2):
+                normed[core, rows, k * COLS : k * COLS + COLS] = chunk[:, core * COLS : core * COLS + COLS]
         return carry
 
     lax.fori_loop(0, TOKENS // 32, norm_rows, 0)
+
+    k_gather.own()
 
     for load in loads[4:]:
         load.wait()
@@ -313,8 +347,11 @@
     )
 
     k_gather.first_near()
+    v_gather.own()
+    v_gather.start_near()
+    k_gather.own_shard()
     k_gather.first_far()
-    v_gather.own()
+
     def wo_rows(core):
         return pl.ds(pl.multiple_of((p.x * (1 - core) + p.y * core) * 32, 32), 32)
 
@@ -327,37 +364,22 @@
     pltpu.make_async_copy(wo_hbm.at[wo_rows(p.c), lanes_of(f, COLS)], wo.at[f, wo_rows(p.c)], pair_sem.at[5]).start()
     lax.fori_loop(1, NF, send_wo, 0)
 
-    wait_bytes(q_recv, pair_sem.at[3])
-    query = q_recv[pl.ds(0, 32), :]
-    for g in range(1, NF):
-        query += q_recv[pl.ds(g * 32, 32), :]
-    query = query * lax.rsqrt(mean_square(query) + EPS) * q_gain[...].astype(F32)
-    row32 = lax.broadcasted_iota(jnp.int32, (32, 128), 0)
-
-    def pooled_angle(table):
-        start = LEAST_LAST // 8 * 8
-        rows = table[pl.ds(start, MOST_LAST + 1 - start), :]
-        here = lax.broadcasted_iota(jnp.int32, rows.shape, 0) == last - start
-        first = jnp.sum(jnp.where(here, rows, 0.0), axis=0, keepdims=True)
-        return jnp.where(row32 < 16, first, table[pl.ds(TOKENS - 1, 1), :])
-
-    query = query * pooled_angle(cos_t) + pltpu.roll(query, 64, 1) * pooled_angle(sin_t)
-    group = row32 % 16 // 4
-    q_block = jnp.concatenate(
-        [jnp.where(group == g, query, 0.0) for g in range(KEY_VALUE_HEADS)], axis=1
-    ).astype(BF16)
-
-    k_gather.second_near()
+    k_gather.second_near((0,))
     v_gather.first_near()
+    k_gather.second_near((3, 1))
+    v_gather.own_shard()
     v_gather.first_far()
+    k_gather.second_near((2,))
+    k_gather.near()
+    v_gather.second_near((0,))
     k_gather.second_far()
 
     key_gain = k_gain[...].astype(F32)
 
     def half_product(w, core, rows):
         return jnp.dot(
-            normed[rows, lanes_of(core, WIDTH // 2)],
-            w[pl.ds(core * 8, 8)].reshape(WIDTH // 2, 512),
+            normed[core, rows, :],
+            w[core].reshape(WIDTH // 2, 512),
             preferred_element_type=F32,
         )
 
@@ -371,7 +393,7 @@
     for i in range(2):
         rows = pl.ds(i * 256, 256)
         sim[rows, :] += half_product(wk, 1 - p.c, rows)
-    v_gather.second_near((0,))
+    v_gather.second_near((3, 1))
 
     def key_rows(i, carry):
         rows = pl.ds(pl.multiple_of(i * 128, 128), 128)
@@ -383,6 +405,26 @@
         return carry
 
     lax.fori_loop(0, TOKENS // 128, key_rows, 0)
+    wait_bytes(q_recv, pair_sem.at[3])
+    query = q_recv[pl.ds(0, 32), :]
+    for g in range(1, NF):
+        query += q_recv[pl.ds(g * 32, 32), :]
+    query = query * lax.rsqrt(mean_square(query) + EPS) * q_gain[...].astype(F32)
+    row32 = lax.broadcasted_iota(jnp.int32, (32, 128), 0)
+
+    def pooled_angle(table):
+        start = LEAST_LAST // 8 * 8
+        rows = table[pl.ds(start, MOST_LAST + 1 - start), :]
+        here = lax.broadcasted_iota(jnp.int32, rows.shape, 0) == last - start
+        first = jnp.sum(jnp.where(here, rows, 0.0), axis=0, keepdims=True)
+        return jnp.where(row32 < 16, first, table[pl.ds(TOKENS - 1, 1), :])
+
+    query = query * pooled_angle(cos_t) + pltpu.roll(query, 64, 1) * pooled_angle(sin_t)
+    group = row32 % 16 // 4
+    q_block = jnp.concatenate(
+        [jnp.where(group == g, query, 0.0) for g in range(KEY_VALUE_HEADS)], axis=1
+    ).astype(BF16)
+
     scores = lax.dot_general(q_block, keys[...], (((1,), (1,)), ((), ())), preferred_element_type=F32)
     scores = scores * (1.0 / math.sqrt(HEAD_SIZE))
     token = lax.broadcasted_iota(jnp.int32, scores.shape, 1)
@@ -391,7 +433,8 @@
     weights = jnp.where(inside, jnp.exp(scores), 0.0)
     probs = (weights / jnp.sum(weights, axis=1, keepdims=True)).astype(BF16)
 
-    v_gather.second_near((3, 1, 2))
+    v_gather.second_near((2,))
+    v_gather.near()
     v_gather.second_far()
     own_wo = wo.at[:, wo_rows(p.c)]
     wait_bytes(own_wo, pair_sem.at[5])
@@ -478,8 +521,8 @@
 
     def half_scores(core, i):
         return lax.dot_general(
-            everyone[pl.ds(i * 8, 8), :, lanes_of(core, WIDTH // 2)].reshape(256, WIDTH // 2),
-            everyone[:, :, lanes_of(core, WIDTH // 2)].reshape(TEXTS, WIDTH // 2),
+            everyone[core, pl.ds(i * 8, 8)].reshape(256, WIDTH // 2),
+            everyone[core].reshape(TEXTS, WIDTH // 2),
             (((1,), (1,)), ((), ())),
             preferred_element_type=F32,
         )
@@ -524,13 +567,15 @@
     for n, item in enumerate(high + low):
         stack = jnp.where(row16 == n, item, stack)
     stack = stack.astype(BF16)
-    for n in range(4):
-        part = jnp.dot(
-            stack,
-            everyone[:, :, n * 1024 : n * 1024 + 1024].reshape(TEXTS, 1024),
-            preferred_element_type=F32,
-        )
-        grad_out[:, n * 1024 : n * 1024 + 1024] = (part[0:2] + part[2:4]) * (1.0 / TEMPER)
+    for core in range(2):
+        for n in range(2):
+            part = jnp.dot(
+                stack, everyone[core, :, :, n * 1024 : n * 1024 + 1024].reshape(TEXTS, 1024), preferred_element_type=F32
+            )
+            part = (part[0:2] + part[2:4]) * (1.0 / TEMPER)
+            for m in range(4):
+                lane = ((n * 4 + m) * 2 + core) * COLS
+                grad_out[:, lane : lane + COLS] = part[:, m * COLS : m * COLS + COLS]
 
     for gather in (k_gather, v_gather, u_gather):
         gather.drain()
@@ -551,7 +596,8 @@
     smem = pl.BlockSpec(memory_space=pltpu.SMEM)
     hbm = pl.BlockSpec(memory_space=pltpu.HBM)
     dma = pltpu.SemaphoreType.DMA
-    gather_sems = [dma, dma, dma, dma, dma, dma, dma((4,)), dma((4, 4))]
+    plane_sems = [dma, dma, dma, dma((4,)), dma((4, 4))]
+    weight_sems = [dma, dma, dma, dma((2,)), dma] + plane_sems
     grad, loss = pl.pallas_call(
         kernel,
         out_shape=(
@@ -562,10 +608,11 @@
         out_specs=(vmem, vmem),
         scratch_shapes=[
             pltpu.VMEM((TOKENS, WIDTH), BF16),
-            pltpu.VMEM((TOKENS, WIDTH), BF16),
-            pltpu.VMEM((NF, ND, 16, 512), BF16),
-            pltpu.VMEM((NF, ND, 16, 512), BF16),
-            pltpu.VMEM((ND, 32, WIDTH), BF16),
+            pltpu.VMEM((2, TOKENS, WIDTH // 2), BF16),
+            pltpu.VMEM((1, WIDTH), F32),
+            pltpu.VMEM((2, 8, ND, 16, 512), BF16),
+            pltpu.VMEM((2, 8, ND, 16, 512), BF16),
+            pltpu.VMEM((2, ND, 32, WIDTH // 2), BF16),
             pltpu.VMEM((COLS, 2048), BF16),
             pltpu.VMEM((NF, 128, COLS), BF16),
             pltpu.VMEM((TOKENS, HEAD_SIZE), F32),
@@ -588,7 +635,9 @@
             dma((7,)),
             dma((14,)),
         ]
-        + gather_sems * 3,
+        + weight_sems * 2
+        + [dma, dma]
+        + plane_sems,
         compiler_params=pltpu.CompilerParams(
             collective_id=0, has_side_effects=True, vmem_limit_bytes=60 * 1024 * 1024
         ),
@@ -598,8 +647,8 @@
         stream,
         norm_gain,
         w_query,
-        key_weight,
-        value_weight,
+        key_weight.reshape(ND, 16, 512),
+        value_weight.reshape(ND, 16, 512),
         w_out,
         q_gain.reshape(1, HEAD_SIZE),
         key_norm_gain.reshape(1, HEAD_SIZE),

time: 87.6 us -> 83.7 us (0.955)
  Pallas kernels: 83.6 us -> 79.7 us
    pallas_call x1, Pallas kernels: 83.6 us -> 79.7 us  [local(): pl.pallas_call(kernel, out_shape=(jax.ShapeDtypeStruct((2, WIDTH), F32),...]
where the time goes in v3:
time: 83.7 us; the launch traced here: 83.5 us
  Pallas kernels  79.7 us (95%)
  between operations  2.4 us (3%)
  local copies, waits for them, and re-layouts  1.38 us (2%)
    pallas_call x1, Pallas kernels, local(): pl.pallas_call(kernel, out_shape=(jax.ShapeDtypeStruct((2, WIDTH), F32),...  79.7 us

profile of v3, /device:TPU:1, one launch (start us, length us, event | category | flops | bytes accessed | tf_op | source)
XLA Modules:
  0.0 83.5 jit_solution(4516235990963765757)
XLA Ops:
  0.6 79.7 %shard_map.140 = (f32[2,4096]{1,0:T(2,128)}, f32[1,1]{1,0:T(1,128)}) custom-call(s32[1,2]{1,0:T(1,128)} %lengths.1, s32[1,2]{1,0:T(1,128)} %bitcast.8, bf16[512,4096]{1,0:T(8,128)(2,1)} %stream_hbm.1, bf16[4096]{0:T(1024)(128)(2,1)} %norm_gain.1, bf16[256,2048]{1,0:T(8,128)(2,1)} %wq_hbm.1, bf16[16,16,512]{2,1,0:T(8,128)(2,1)} %bitcast.6, ...), custom_call_target="tpu_custom_call" | custom-call | tf_op jit(solution)/shard_map/pallas_call | solution.py:601
  80.4 1.4 %copy.17 = f32[2,4096]{1,0:T(2,128)} copy(f32[2,4096]{1,0:T(2,128)} %get-tuple-element.8) | data formatting | bytes 65536

commit v4 on v3

--- a/solution.py
+++ b/solution.py
@@ -502,6 +502,14 @@
 
     pltpu.make_async_copy(c_send, c_recv.at[rows_of(d, 8)], pair_sem.at[11]).start()
     lax.fori_loop(1, ND, send_factor, 0)
+
+    k_gather.drain()
+    v_gather.drain()
+    wait_bytes(pool_send.at[pl.ds(0, 15 * 8)], pair_sem.at[0])
+    wait_bytes(q_send.at[pl.ds(0, 15 * 32)], pair_sem.at[2])
+    wait_bytes(wo.at[pl.ds(0, 15), pl.ds(0, 32)], pair_sem.at[4])
+    wait_bytes(wo.at[pl.ds(0, 12)], pair_sem.at[12])
+    wait_bytes(mix_recv.at[pl.ds(0, 15)], pair_sem.at[6])
 
     u_gather.first_near()
     u_gather.first_far()
@@ -577,13 +585,7 @@
                 lane = ((n * 4 + m) * 2 + core) * COLS
                 grad_out[:, lane : lane + COLS] = part[:, m * COLS : m * COLS + COLS]
 
-    for gather in (k_gather, v_gather, u_gather):
-        gather.drain()
-    wait_bytes(pool_send.at[pl.ds(0, 15 * 8)], pair_sem.at[0])
-    wait_bytes(q_send.at[pl.ds(0, 15 * 32)], pair_sem.at[2])
-    wait_bytes(wo.at[pl.ds(0, 15), pl.ds(0, 32)], pair_sem.at[4])
-    wait_bytes(wo.at[pl.ds(0, 12)], pair_sem.at[12])
-    wait_bytes(mix_recv.at[pl.ds(0, 15)], pair_sem.at[6])
+    u_gather.drain()
     wait_bytes(ab_recv.at[pl.ds(0, 15 * 8)], pair_sem.at[8])
     wait_bytes(c_recv.at[pl.ds(0, 15 * 8)], pair_sem.at[10])
 

time: 83.7 us -> 83.7 us (level)
  no operation moved by 1% of the time
where the time goes in v4:
time: 83.7 us; the launch traced here: 83.5 us
  Pallas kernels  79.7 us (95%)
  between operations  2.4 us (3%)
  local copies, waits for them, and re-layouts  1.38 us (2%)
    pallas_call x1, Pallas kernels, local(): pl.pallas_call(kernel, out_shape=(jax.ShapeDtypeStruct((2, WIDTH), F32),...  79.7 us

profile of v4, /device:TPU:1, one launch (start us, length us, event | category | flops | bytes accessed | tf_op | source)
XLA Modules:
  0.0 83.5 jit_solution(8500671371433095566)
XLA Ops:
  0.6 79.7 %shard_map.140 = (f32[2,4096]{1,0:T(2,128)}, f32[1,1]{1,0:T(1,128)}) custom-call(s32[1,2]{1,0:T(1,128)} %lengths.1, s32[1,2]{1,0:T(1,128)} %bitcast.8, bf16[512,4096]{1,0:T(8,128)(2,1)} %stream_hbm.1, bf16[4096]{0:T(1024)(128)(2,1)} %norm_gain.1, bf16[256,2048]{1,0:T(8,128)(2,1)} %wq_hbm.1, bf16[16,16,512]{2,1,0:T(8,128)(2,1)} %bitcast.6, ...), custom_call_target="tpu_custom_call" | custom-call | tf_op jit(solution)/shard_map/pallas_call | solution.py:603
  80.4 1.4 %copy.17 = f32[2,4096]{1,0:T(2,128)} copy(f32[2,4096]{1,0:T(2,128)} %get-tuple-element.8) | data formatting | bytes 65536

commit v5 on v4

--- a/solution.py
+++ b/solution.py
@@ -239,10 +239,10 @@
 
 
 def kernel(
-    lengths, partner, stream_hbm, norm_gain, wq_hbm, wk_hbm, wv_hbm, wo_hbm, q_gain, k_gain, final_gain,
+    lengths, partner, stream_hbm, norm_hbm, wq_hbm, wk_hbm, wv_hbm, wo_hbm, q_gain, k_gain, final_hbm,
     cos_hbm, sin_hbm,
     grad_out, loss_out,
-    stream, normed, gain_row, wk, wv, everyone, wq, wo, cos_t, sin_t,
+    norm_gain, final_gain, stream, normed, gain_row, wk, wv, everyone, wq, wo, cos_t, sin_t,
     pool_send, pool_recv, q_send, q_recv, mix_send, mix_recv, mix_f32,
     ab_send, ab_recv, c_send, c_recv, u_send, keys, values, sim,
     load_sem, pair_sem,
@@ -261,6 +261,8 @@
         for i in range(4)
     ]
     loads += [
+        pltpu.make_async_copy(norm_hbm, norm_gain, load_sem.at[7]),
+        pltpu.make_async_copy(final_hbm, final_gain, load_sem.at[8]),
         pltpu.make_async_copy(wq_hbm, wq, load_sem.at[4]),
         pltpu.make_async_copy(cos_hbm, cos_t, load_sem.at[5]),
         pltpu.make_async_copy(sin_hbm, sin_t, load_sem.at[6]),
@@ -284,7 +286,7 @@
 
     k_gather.start()
 
-    for load in loads[:4]:
+    for load in loads[:5]:
         load.wait()
     last = lengths[0, 0] - 1
     gain = norm_gain[...].astype(F32).reshape(1, WIDTH)
@@ -325,7 +327,7 @@
 
     k_gather.own()
 
-    for load in loads[4:]:
+    for load in loads[5:]:
         load.wait()
     wait_bytes(pool_recv, pair_sem.at[1])
 
@@ -606,9 +608,11 @@
             jax.ShapeDtypeStruct((2, WIDTH), F32),
             jax.ShapeDtypeStruct((1, 1), F32),
         ),
-        in_specs=[smem, smem, hbm, vmem, hbm, hbm, hbm, hbm, vmem, vmem, vmem, hbm, hbm],
+        in_specs=[smem, smem, hbm, hbm, hbm, hbm, hbm, hbm, vmem, vmem, hbm, hbm, hbm],
         out_specs=(vmem, vmem),
         scratch_shapes=[
+            pltpu.VMEM((WIDTH,), BF16),
+            pltpu.VMEM((WIDTH,), BF16),
             pltpu.VMEM((TOKENS, WIDTH), BF16),
             pltpu.VMEM((2, TOKENS, WIDTH // 2), BF16),
             pltpu.VMEM((1, WIDTH), F32),
@@ -634,7 +638,7 @@
             pltpu.VMEM((TOKENS, 512), BF16),
             pltpu.VMEM((TOKENS, 512), BF16),
             pltpu.VMEM((TEXTS, TEXTS), F32),
-            dma((7,)),
+            dma((11,)),
             dma((14,)),
         ]
         + weight_sems * 2

time: 83.7 us -> 83.6 us (level)
  no operation moved by 1% of the time
where the time goes in v5:
time: 83.6 us; the launch traced here: 83.4 us
  Pallas kernels  79.7 us (95%)
  between operations  2.4 us (3%)
  local copies, waits for them, and re-layouts  1.38 us (2%)
    pallas_call x1, Pallas kernels, local(): pl.pallas_call(kernel, out_shape=(jax.ShapeDtypeStruct((2, WIDTH), F32),...  79.7 us

profile of v5, /device:TPU:1, one launch (start us, length us, event | category | flops | bytes accessed | tf_op | source)
XLA Modules:
  0.0 83.4 jit_solution(13255055051009651510)
XLA Ops:
  0.6 79.7 %shard_map.140 = (f32[2,4096]{1,0:T(2,128)}, f32[1,1]{1,0:T(1,128)}) custom-call(s32[1,2]{1,0:T(1,128)} %lengths.1, s32[1,2]{1,0:T(1,128)} %bitcast.8, bf16[512,4096]{1,0:T(8,128)(2,1)} %stream_hbm.1, bf16[4096]{0:T(1024)(128)(2,1)} %norm_hbm.1, bf16[256,2048]{1,0:T(8,128)(2,1)} %wq_hbm.1, bf16[16,16,512]{2,1,0:T(8,128)(2,1)} %bitcast.6, ...), custom_call_target="tpu_custom_call" | custom-call | tf_op jit(solution)/shard_map/pallas_call | solution.py:605
  80.3 1.4 %copy.17 = f32[2,4096]{1,0:T(2,128)} copy(f32[2,4096]{1,0:T(2,128)} %get-tuple-element.8) | data formatting | bytes 65536
